TPU v7x, 32 devices: a whole 2x2x4 slice. The times are simulated.
32 devices in a mesh: clip: 4 (over y, core), ctx: 8 (over z, x).
Axes of the slice: x: 2, y: 2, z: 4, core: 2. Of those that a mesh axis runs over, the one named last changes fastest.
Arguments:
- queries: bfloat16 [4096, 4096], P(('clip', 'ctx')), parts along dimension 0, may hold values from -48 to 48
- key_rows: bfloat16 [4096, 4096], P(('clip', 'ctx')), parts along dimension 0, may hold values from -48 to 48
- values: bfloat16 [4096, 4096], P(('clip', 'ctx')), parts along dimension 0, may hold values from -6 to 6
- tangent_queries: bfloat16 [4096, 4096], P(('clip', 'ctx')), parts along dimension 0, may hold values from -6 to 6
- tangent_keys: bfloat16 [4096, 4096], P(('clip', 'ctx')), parts along dimension 0, may hold values from -6 to 6
- tangent_values: bfloat16 [4096, 4096], P(('clip', 'ctx')), parts along dimension 0, may hold values from -6 to 6
Outputs:
- attended: bfloat16 [4096, 4096], P(('clip', 'ctx')), parts along dimension 0
- tangent_output: bfloat16 [4096, 4096], P(('clip', 'ctx')), parts along dimension 0
There are 4 independent parts, one for each index of `clip`. A program takes and returns all parts, laid end to end along the dimension named above; each array names one. Nothing has to cross between parts.
All inputs are finite; a program needn't handle non-finite values.
Results may differ from a plain program's by a relative error of at most 0.012.
Values may be sent and summed in bfloat16 or wider, within the bound.
A program may use at most 64 MiB of HBM per device.

v0:
```python
import jax
import jax.numpy as jnp
from jax import lax
from jax.sharding import PartitionSpec as P

HD = 128


def split_blocks(array, block):
    return array.reshape(array.shape[0] // block, block, array.shape[1], array.shape[2])


def probs_block(query_block, key_all, scale):
    scores = (
        jnp.einsum("qhd,khd->hqk", query_block, key_all, preferred_element_type=jnp.float32) * scale
    )
    top = jnp.max(scores, axis=-1, keepdims=True)
    raised = jnp.exp(scores - top)
    return raised / jnp.sum(raised, axis=-1, keepdims=True)


def primal_block(prob_half, value_all):
    return jnp.einsum("hqk,khd->qhd", prob_half, value_all, preferred_element_type=jnp.float32)


def tangent_block(
    query_block,
    tquery_block,
    probs,
    prob_half,
    key_all,
    value_all,
    tkey_all,
    tvalue_all,
    primal,
    scale,
):
    dscores = (
        jnp.einsum("qhd,khd->hqk", tquery_block, key_all, preferred_element_type=jnp.float32)
        + jnp.einsum("qhd,khd->hqk", query_block, tkey_all, preferred_element_type=jnp.float32)
    ) * scale
    weighted = probs * dscores
    correction = jnp.transpose(jnp.sum(weighted, axis=-1, keepdims=True), (1, 0, 2))
    weight_half = weighted.astype(jnp.bfloat16)
    return (
        jnp.einsum("hqk,khd->qhd", weight_half, value_all, preferred_element_type=jnp.float32)
        + jnp.einsum("hqk,khd->qhd", prob_half, tvalue_all, preferred_element_type=jnp.float32)
        - correction * primal
    )


def joined(blocks, total):
    return blocks.reshape(total, 1, blocks.shape[2], blocks.shape[3])


def body(queries, key_rows, values, tangent_queries, tangent_keys, tangent_values):
    groups = lax.axis_size("ctx")
    tok_rows = queries.shape[0]
    width = queries.shape[1]
    head_count = width // (groups * HD)

    def by_group(array):
        return array.reshape(tok_rows, groups, head_count, HD)

    scale = HD ** (-0.5)
    primal_x = (
        lax.all_to_all(by_group(queries), "ctx", split_axis=1, concat_axis=0, tiled=True),
        lax.all_to_all(by_group(key_rows), "ctx", split_axis=1, concat_axis=0, tiled=True),
        lax.all_to_all(by_group(values), "ctx", split_axis=1, concat_axis=0, tiled=True),
    )
    query_all, key_all, value_all = [piece[:, 0] for piece in primal_x]
    total = query_all.shape[0]
    block = min(512, total)
    query_blocks = split_blocks(query_all, block)

    def primal_only(query_block):
        probs = probs_block(query_block, key_all, scale)
        return primal_block(probs.astype(jnp.bfloat16), value_all)

    primal_blocks = lax.map(primal_only, query_blocks)
    tangent_x = (
        lax.all_to_all(by_group(tangent_queries), "ctx", split_axis=1, concat_axis=0, tiled=True),
        lax.all_to_all(by_group(tangent_keys), "ctx", split_axis=1, concat_axis=0, tiled=True),
        lax.all_to_all(by_group(tangent_values), "ctx", split_axis=1, concat_axis=0, tiled=True),
    )
    tquery_all, tkey_all, tvalue_all = [piece[:, 0] for piece in tangent_x]

    def tangent_only(triple):
        query_block, tquery_block, primal = triple
        probs = probs_block(query_block, key_all, scale)
        prob_half = probs.astype(jnp.bfloat16)
        tangent = tangent_block(
            query_block,
            tquery_block,
            probs,
            prob_half,
            key_all,
            value_all,
            tkey_all,
            tvalue_all,
            primal,
            scale,
        )
        return tangent.astype(jnp.bfloat16)

    tangent_blocks = lax.map(
        tangent_only, (query_blocks, split_blocks(tquery_all, block), primal_blocks)
    )
    out_half = joined(primal_blocks.astype(jnp.bfloat16), total)
    tangent_half = joined(tangent_blocks, total)
    attended, tangent_output = (
        lax.all_to_all(out_half, "ctx", split_axis=0, concat_axis=1, tiled=True),
        lax.all_to_all(tangent_half, "ctx", split_axis=0, concat_axis=1, tiled=True),
    )
    return (attended.reshape(tok_rows, width), tangent_output.reshape(tok_rows, width))


def solution(mesh):
    return jax.shard_map(
        body,
        mesh=mesh,
        in_specs=(
            P(("clip", "ctx"), None),
            P(("clip", "ctx"), None),
            P(("clip", "ctx"), None),
            P(("clip", "ctx"), None),
            P(("clip", "ctx"), None),
            P(("clip", "ctx"), None),
        ),
        out_specs=(P(("clip", "ctx"), None), P(("clip", "ctx"), None)),
        check_vma=False,
    )
```

profile of v0, /device:TPU:11, one launch (start us, length us, event | category | flops | bytes accessed | tf_op | source)
XLA Modules:
  0.0 289.6 jit_solution(18424839567918141479)
XLA Ops:
  0.6 1.7 copy.57
  2.4 1.3 copy.58
  3.7 5.7 %all-to-all-start.1 = ((bf16[128,8,4,128]{3,0,2,1:T(8,128)(2,1)}), bf16[128,8,4,128]{3,0,2,1:T(8,128)(2,1)S(1)}, u32[]{:S(2)}, u32[]{:S(2)}) async-start(bf16[128,8,4,128]{3,0,2,1:T(8,128)(2,1)} %copy.58), calls=%async_computation.1 | async-start | bytes 2097152 | tf_op jit(solution)/shard_map/all_to_all | solution.py:68
  9.3 1.6 copy.60
  10.9 1.3 copy.61
  12.3 20.3 %all-to-all-done.1 = bf16[128,8,4,128]{3,0,2,1:T(8,128)(2,1)S(1)} async-done(((bf16[128,8,4,128]{3,0,2,1:T(8,128)(2,1)}), bf16[128,8,4,128]{3,0,2,1:T(8,128)(2,1)S(1)}, u32[]{:S(2)}, u32[]{:S(2)}) %all-to-all-start.1) | async-done | bytes 1048608 | tf_op jit(solution)/shard_map/all_to_all | solution.py:68
  32.5 6.3 %all-to-all-start.2 = ((bf16[128,8,4,128]{3,0,2,1:T(8,128)(2,1)}), bf16[128,8,4,128]{3,0,2,1:T(8,128)(2,1)S(1)}, u32[]{:S(2)}, u32[]{:S(2)}) async-start(bf16[128,8,4,128]{3,0,2,1:T(8,128)(2,1)} %copy.61), calls=%async_computation.2 | async-start | bytes 2097152 | tf_op jit(solution)/shard_map/all_to_all | solution.py:69
  38.9 1.3 copy.55
  40.2 21.9 %all-to-all-done.2 = bf16[128,8,4,128]{3,0,2,1:T(8,128)(2,1)S(1)} async-done(((bf16[128,8,4,128]{3,0,2,1:T(8,128)(2,1)}), bf16[128,8,4,128]{3,0,2,1:T(8,128)(2,1)S(1)}, u32[]{:S(2)}, u32[]{:S(2)}) %all-to-all-start.2) | async-done | bytes 1048608 | tf_op jit(solution)/shard_map/all_to_all | solution.py:69
  62.1 6.3 %all-to-all-start = ((bf16[128,8,4,128]{0,3,2,1:T(8,128)(2,1)}), bf16[128,8,4,128]{0,3,2,1:T(8,128)(2,1)S(1)}, u32[]{:S(2)}, u32[]{:S(2)}) async-start(bf16[128,8,4,128]{0,3,2,1:T(8,128)(2,1)} %bitcast.159), calls=%async_computation | async-start | bytes 2097152 | tf_op jit(solution)/shard_map/all_to_all | solution.py:67
  68.5 2.3 copy.68
  70.7 21.0 %all-to-all-done = bf16[128,8,4,128]{0,3,2,1:T(8,128)(2,1)S(1)} async-done(((bf16[128,8,4,128]{0,3,2,1:T(8,128)(2,1)}), bf16[128,8,4,128]{0,3,2,1:T(8,128)(2,1)S(1)}, u32[]{:S(2)}, u32[]{:S(2)}) %all-to-all-start) | async-done | bytes 1048608 | tf_op jit(solution)/shard_map/all_to_all | solution.py:67
  91.7 6.3 %all-to-all-start.4 = ((bf16[128,8,4,128]{0,3,2,1:T(8,128)(2,1)}), bf16[128,8,4,128]{0,3,2,1:T(8,128)(2,1)}, u32[]{:S(2)}, u32[]{:S(2)}) async-start(bf16[128,8,4,128]{0,3,2,1:T(8,128)(2,1)} %bitcast.158), calls=%async_computation.4 | async-start | bytes 2097152 | tf_op jit(solution)/shard_map/all_to_all | solution.py:82
  98.0 2.3 copy.70
  100.3 2.3 copy.71
  102.6 18.7 %all-to-all-done.4 = bf16[128,8,4,128]{0,3,2,1:T(8,128)(2,1)} async-done(((bf16[128,8,4,128]{0,3,2,1:T(8,128)(2,1)}), bf16[128,8,4,128]{0,3,2,1:T(8,128)(2,1)}, u32[]{:S(2)}, u32[]{:S(2)}) %all-to-all-start.4) | async-done | bytes 1048608 | tf_op jit(solution)/shard_map/all_to_all | solution.py:82
  121.2 6.5 %all-to-all-start.5 = ((bf16[128,8,4,128]{3,0,2,1:T(8,128)(2,1)}), bf16[128,8,4,128]{3,0,2,1:T(8,128)(2,1)}, u32[]{:S(2)}, u32[]{:S(2)}) async-start(bf16[128,8,4,128]{3,0,2,1:T(8,128)(2,1)} %copy.71), calls=%async_computation.5 | async-start | bytes 2097152 | tf_op jit(solution)/shard_map/all_to_all | solution.py:83
  127.7 2.3 copy.73
  130.0 2.3 copy.74
  134.0 1.6 copy.69
  135.7 2.3 copy.62
  138.0 12.8 %all-to-all-done.5 = bf16[128,8,4,128]{3,0,2,1:T(8,128)(2,1)} async-done(((bf16[128,8,4,128]{3,0,2,1:T(8,128)(2,1)}), bf16[128,8,4,128]{3,0,2,1:T(8,128)(2,1)}, u32[]{:S(2)}, u32[]{:S(2)}) %all-to-all-start.5) | async-done | bytes 1048608 | tf_op jit(solution)/shard_map/all_to_all | solution.py:83
  150.9 6.5 %all-to-all-start.6 = ((bf16[128,8,4,128]{3,0,2,1:T(8,128)(2,1)}), bf16[128,8,4,128]{3,0,2,1:T(8,128)(2,1)S(1)}, u32[]{:S(2)}, u32[]{:S(2)}) async-start(bf16[128,8,4,128]{3,0,2,1:T(8,128)(2,1)} %copy.74), calls=%async_computation.6 | async-start | bytes 2097152 | tf_op jit(solution)/shard_map/all_to_all | solution.py:84
  157.3 2.3 copy.72
  159.7 25.5 %while.20 = (s32[]{:T(128)}, f32[2,512,4,128]{3,1,2,0:T(8,128)}, bf16[2,512,4,128]{3,1,2,0:T(8,128)(2,1)}, bf16[1024,4,128]{2,0,1:T(8,128)(2,1)S(1)}, bf16[1024,4,128]{2,0,1:T(8,128)(2,1)}, /*index=5*/s32[]{:T(128)}) while((s32[]{:T(128)}, f32[2,512,4,128]{3,1,2,0:T(8,128)}, bf16[2,512,4,128]{3,1,2,0:T(8,128)(2,1)}, ...), condition=%wide.region_3.4_spmd, body=%wide.region_0.3_spmd.sunk | while | flops 1084228608 | bytes 20464708 | solution.py:80
  159.7 6.8 %fusion.121 = (f32[4,512]{1,0:T(4,128)S(1)}, f32[4,512,1024]{2,1,0:T(8,128)}) fusion(bf16[1024,4,128]{2,0,1:T(8,128)(2,1)S(1)} %get-tuple-element.289, bf16[2,512,4,128]{3,1,2,0:T(8,128)(2,1)} %get-tuple-element.288, s32[]{:T(128)} %get-tuple-element.280), kind=kOutput, calls=%fused_computation.53.clone.1 | convolution fusion | flops 543163392 | bytes 9970176 | tf_op jit(solution)/shard_map/while/body/eval_jaxpr/sub | solution.py:18
  166.5 6.0 %fusion.122 = f32[2,512,4,128]{3,1,2,0:T(8,128)} fusion(f32[2,512,4,128]{3,1,2,0:T(8,128)} %get-tuple-element.281, s32[]{:T(128)} %get-tuple-element.280, bf16[1024,4,128]{2,0,1:T(8,128)(2,1)} %get-tuple-element.290, f32[4,512,1024]{2,1,0:T(8,128)} %get-tuple-element.259, f32[4,512]{1,0:T(4,128)S(1)} %get-tuple-element.260), kind=kOutput, calls=%fused_computation.8.clone.1 | convolution fusion | flops 541065216 | bytes 10494464 | tf_op jit(solution)/shard_map/while/body/eval_jaxpr/hqk,khd->qhd/dot_general | solution.py:23
  172.5 6.8 %fusion.121 = (f32[4,512]{1,0:T(4,128)S(1)}, f32[4,512,1024]{2,1,0:T(8,128)}) fusion(bf16[1024,4,128]{2,0,1:T(8,128)(2,1)S(1)} %get-tuple-element.289, bf16[2,512,4,128]{3,1,2,0:T(8,128)(2,1)} %get-tuple-element.288, s32[]{:T(128)} %get-tuple-element.280), kind=kOutput, calls=%fused_computation.53.clone.1 | convolution fusion | flops 543163392 | bytes 9970176 | tf_op jit(solution)/shard_map/while/body/eval_jaxpr/sub | solution.py:18
  179.3 5.9 %fusion.122 = f32[2,512,4,128]{3,1,2,0:T(8,128)} fusion(f32[2,512,4,128]{3,1,2,0:T(8,128)} %get-tuple-element.281, s32[]{:T(128)} %get-tuple-element.280, bf16[1024,4,128]{2,0,1:T(8,128)(2,1)} %get-tuple-element.290, f32[4,512,1024]{2,1,0:T(8,128)} %get-tuple-element.259, f32[4,512]{1,0:T(4,128)S(1)} %get-tuple-element.260), kind=kOutput, calls=%fused_computation.8.clone.1 | convolution fusion | flops 541065216 | bytes 10494464 | tf_op jit(solution)/shard_map/while/body/eval_jaxpr/hqk,khd->qhd/dot_general | solution.py:23
  186.3 40.0 %while.21 = (s32[]{:T(128)}, bf16[2,512,4,128]{3,1,0,2:T(8,128)(2,1)}, bf16[2,512,4,128]{3,1,2,0:T(8,128)(2,1)}, bf16[1024,4,128]{2,0,1:T(8,128)(2,1)S(1)}, bf16...) while((s32[]{:T(128)}, ...), condition=%wide.region_8.9_spmd, body=%wide.region_4.8_spmd.sunk | while | flops 2708470784 | bytes 86025456 | solution.py:106
  186.3 6.9 %fusion.132 = (f32[4,512]{1,0:T(4,128)S(1)}, f32[4,512,1024]{2,1,0:T(8,128)}) fusion(bf16[1024,4,128]{2,0,1:T(8,128)(2,1)S(1)} %get-tuple-element.315, bf16[2,512,4,128]{3,1,2,0:T(8,128)(2,1)} %get-tuple-element.314, s32[]{:T(128)} %get-tuple-element.302), kind=kOutput, calls=%fused_computation.54.clone.1 | convolution fusion | flops 543163392 | bytes 9970176 | tf_op jit(solution)/shard_map/while/body/eval_jaxpr/sub | solution.py:18
  194.5 4.8 %fusion.135 = (f32[4,512]{1,0:T(4,128)S(1)}, bf16[4,512,1024]{2,1,0:T(8,128)(2,1)S(1)}) fusion(f32[4,512,1024]{2,1,0:T(8,128)S(1)} %fusion.134, bf16[1024,4,128]{2,0,1:T(8,128)(2,1)S(1)} %copy-done.5, bf16[2,512,4,128]{3,1,2,0:T(8,128)(2,1)S(1)} %copy-done.3, s32[]{:T(128)} %get-tuple-element.302, f32[4,512,1024]{2,1,0:T(8,128)} %get-tuple-element.270, ...), kind=kOutput, calls=%fused_computation.55.clone.1 | convolution fusion | flops 549451776 | bytes 22560772 | tf_op jit(solution)/shard_map/while/body/eval_jaxpr/qhd,khd->hqk/dot_general | solution.py:40
  199.3 4.9 %fusion.133 = f32[4,512,128]{2,1,0:T(8,128)S(1)} fusion(bf16[1024,4,128]{2,0,1:T(8,128)(2,1)S(1)} %copy-done.6, f32[4,512,1024]{2,1,0:T(8,128)} %get-tuple-element.270, f32[4,512]{1,0:T(4,128)S(1)} %get-tuple-element.271), kind=kOutput, calls=%fused_computation.23.clone.1 | convolution fusion | flops 541065216 | bytes 10493952 | tf_op jit(solution)/shard_map/while/body/eval_jaxpr/hqk,khd->qhd/dot_general | solution.py:47
  204.2 2.1 fusion.136
  206.3 6.9 %fusion.132 = (f32[4,512]{1,0:T(4,128)S(1)}, f32[4,512,1024]{2,1,0:T(8,128)}) fusion(bf16[1024,4,128]{2,0,1:T(8,128)(2,1)S(1)} %get-tuple-element.315, bf16[2,512,4,128]{3,1,2,0:T(8,128)(2,1)} %get-tuple-element.314, s32[]{:T(128)} %get-tuple-element.302), kind=kOutput, calls=%fused_computation.54.clone.1 | convolution fusion | flops 543163392 | bytes 9970176 | tf_op jit(solution)/shard_map/while/body/eval_jaxpr/sub | solution.py:18
  213.2 1.3 fusion.134
  214.5 4.8 %fusion.135 = (f32[4,512]{1,0:T(4,128)S(1)}, bf16[4,512,1024]{2,1,0:T(8,128)(2,1)S(1)}) fusion(f32[4,512,1024]{2,1,0:T(8,128)S(1)} %fusion.134, bf16[1024,4,128]{2,0,1:T(8,128)(2,1)S(1)} %copy-done.5, bf16[2,512,4,128]{3,1,2,0:T(8,128)(2,1)S(1)} %copy-done.3, s32[]{:T(128)} %get-tuple-element.302, f32[4,512,1024]{2,1,0:T(8,128)} %get-tuple-element.270, ...), kind=kOutput, calls=%fused_computation.55.clone.1 | convolution fusion | flops 549451776 | bytes 22560772 | tf_op jit(solution)/shard_map/while/body/eval_jaxpr/qhd,khd->hqk/dot_general | solution.py:40
  219.3 4.9 %fusion.133 = f32[4,512,128]{2,1,0:T(8,128)S(1)} fusion(bf16[1024,4,128]{2,0,1:T(8,128)(2,1)S(1)} %copy-done.6, f32[4,512,1024]{2,1,0:T(8,128)} %get-tuple-element.270, f32[4,512]{1,0:T(4,128)S(1)} %get-tuple-element.271), kind=kOutput, calls=%fused_computation.23.clone.1 | convolution fusion | flops 541065216 | bytes 10493952 | tf_op jit(solution)/shard_map/while/body/eval_jaxpr/hqk,khd->qhd/dot_general | solution.py:47
  224.2 2.1 fusion.136
  226.3 3.0 %copy.79 = bf16[1024,1,4,128]{3,2,1,0:T(4,128)(2,1)} copy(bf16[1024,1,4,128]{3,0,2,1:T(8,128)(2,1)} %bitcast.43) | data formatting | bytes 2097152 | tf_op jit(solution)/shard_map/reshape | solution.py:53
  229.3 5.4 %all-to-all-start.7 = ((bf16[1024,1,4,128]{3,2,1,0:T(4,128)(2,1)}), bf16[1024,1,4,128]{3,2,1,0:T(4,128)(2,1)S(1)}, u32[]{:S(2)}, u32[]{:S(2)}) async-start(bf16[1024,1,4,128]{3,2,1,0:T(4,128)(2,1)} %copy.79), calls=%async_computation.7 | async-start | bytes 2097152 | tf_op jit(solution)/shard_map/all_to_all | solution.py:113
  234.7 1.8 copy.88
  236.5 1.8 copy.65
  238.3 19.6 %all-to-all-done.7 = bf16[1024,1,4,128]{3,2,1,0:T(4,128)(2,1)S(1)} async-done(((bf16[1024,1,4,128]{3,2,1,0:T(4,128)(2,1)}), bf16[1024,1,4,128]{3,2,1,0:T(4,128)(2,1)S(1)}, u32[]{:S(2)}, u32[]{:S(2)}) %all-to-all-start.7) | async-done | bytes 1048608 | tf_op jit(solution)/shard_map/all_to_all | solution.py:113
  257.9 6.3 %all-to-all-start.3 = ((bf16[1024,1,4,128]{3,2,1,0:T(4,128)(2,1)}), bf16[1024,1,4,128]{3,2,1,0:T(4,128)(2,1)S(1)}, u32[]{:S(2)}, u32[]{:S(2)}) async-start(bf16[1024,1,4,128]{3,2,1,0:T(4,128)(2,1)} %copy.65), calls=%async_computation.3 | async-start | bytes 2097152 | tf_op jit(solution)/shard_map/all_to_all | solution.py:112
  265.1 1.3 copy.83
  266.4 21.1 %all-to-all-done.3 = bf16[1024,1,4,128]{3,2,1,0:T(4,128)(2,1)S(1)} async-done(((bf16[1024,1,4,128]{3,2,1,0:T(4,128)(2,1)}), bf16[1024,1,4,128]{3,2,1,0:T(4,128)(2,1)S(1)}, u32[]{:S(2)}, u32[]{:S(2)}) %all-to-all-start.3) | async-done | bytes 1048608 | tf_op jit(solution)/shard_map/all_to_all | solution.py:112
  288.3 1.3 copy.82
  (36 shorter events, 5.8 us)
Async XLA Ops:
  0.6 38.2 %copy-start.2 = (bf16[128,4096]{1,0:T(8,128)(2,1)S(1)}, bf16[128,4096]{1,0:T(8,128)(2,1)}, u32[]{:S(2)}) copy-start(bf16[128,4096]{1,0:T(8,128)(2,1)} %param.10) | copy-start | bytes 3145732
  3.7 28.9 %all-to-all-start.1 = ((bf16[128,8,4,128]{3,0,2,1:T(8,128)(2,1)}), bf16[128,8,4,128]{3,0,2,1:T(8,128)(2,1)S(1)}, u32[]{:S(2)}, u32[]{:S(2)}) async-start(bf16[128,8,4,128]{3,0,2,1:T(8,128)(2,1)} %copy.58), calls=%async_computation.1 | async-start | bytes 2097152 | tf_op jit(solution)/shard_map/all_to_all | solution.py:68
  32.5 29.6 %all-to-all-start.2 = ((bf16[128,8,4,128]{3,0,2,1:T(8,128)(2,1)}), bf16[128,8,4,128]{3,0,2,1:T(8,128)(2,1)S(1)}, u32[]{:S(2)}, u32[]{:S(2)}) async-start(bf16[128,8,4,128]{3,0,2,1:T(8,128)(2,1)} %copy.61), calls=%async_computation.2 | async-start | bytes 2097152 | tf_op jit(solution)/shard_map/all_to_all | solution.py:69
  62.1 70.2 %copy-start = (bf16[128,8,4,128]{3,0,2,1:T(8,128)(2,1)}, bf16[128,8,4,128]{3,0,2,1:T(8,128)(2,1)S(1)}, u32[]{:S(2)}) copy-start(bf16[128,8,4,128]{3,0,2,1:T(8,128)(2,1)S(1)} %all-to-all-done.2) | copy-start | bytes 3145732
  62.1 29.6 %all-to-all-start = ((bf16[128,8,4,128]{0,3,2,1:T(8,128)(2,1)}), bf16[128,8,4,128]{0,3,2,1:T(8,128)(2,1)S(1)}, u32[]{:S(2)}, u32[]{:S(2)}) async-start(bf16[128,8,4,128]{0,3,2,1:T(8,128)(2,1)} %bitcast.159), calls=%async_computation | async-start | bytes 2097152 | tf_op jit(solution)/shard_map/all_to_all | solution.py:67
  91.7 29.5 %all-to-all-start.4 = ((bf16[128,8,4,128]{0,3,2,1:T(8,128)(2,1)}), bf16[128,8,4,128]{0,3,2,1:T(8,128)(2,1)}, u32[]{:S(2)}, u32[]{:S(2)}) async-start(bf16[128,8,4,128]{0,3,2,1:T(8,128)(2,1)} %bitcast.158), calls=%async_computation.4 | async-start | bytes 2097152 | tf_op jit(solution)/shard_map/all_to_all | solution.py:82
  121.2 29.6 %all-to-all-start.5 = ((bf16[128,8,4,128]{3,0,2,1:T(8,128)(2,1)}), bf16[128,8,4,128]{3,0,2,1:T(8,128)(2,1)}, u32[]{:S(2)}, u32[]{:S(2)}) async-start(bf16[128,8,4,128]{3,0,2,1:T(8,128)(2,1)} %copy.71), calls=%async_computation.5 | async-start | bytes 2097152 | tf_op jit(solution)/shard_map/all_to_all | solution.py:83
  150.9 34.3 %all-to-all-start.6 = ((bf16[128,8,4,128]{3,0,2,1:T(8,128)(2,1)}), bf16[128,8,4,128]{3,0,2,1:T(8,128)(2,1)S(1)}, u32[]{:S(2)}, u32[]{:S(2)}) async-start(bf16[128,8,4,128]{3,0,2,1:T(8,128)(2,1)} %copy.74), calls=%async_computation.6 | async-start | bytes 2097152 | tf_op jit(solution)/shard_map/all_to_all | solution.py:84
  186.3 8.2 %copy-start.3 = (bf16[2,512,4,128]{3,1,2,0:T(8,128)(2,1)S(1)}, bf16[2,512,4,128]{3,1,2,0:T(8,128)(2,1)}, u32[]{:S(2)}) copy-start(bf16[2,512,4,128]{3,1,2,0:T(8,128)(2,1)} %get-tuple-element.314) | copy-start | bytes 3145732 | tf_op jit(solution)/shard_map/while
  193.2 1.3 copy-start.5
  194.5 4.8 %copy-start.6 = (bf16[1024,4,128]{2,0,1:T(8,128)(2,1)S(1)}, bf16[1024,4,128]{2,0,1:T(8,128)(2,1)}, u32[]{:S(2)}) copy-start(bf16[1024,4,128]{2,0,1:T(8,128)(2,1)} %get-tuple-element.319) | copy-start | bytes 3145732 | tf_op jit(solution)/shard_map/while
  199.3 4.9 %copy-start.1 = (f32[2,512,4,128]{3,1,2,0:T(8,128)S(1)}, f32[2,512,4,128]{3,1,2,0:T(8,128)}, u32[]{:S(2)}) copy-start(f32[2,512,4,128]{3,1,2,0:T(8,128)} %get-tuple-element.320) | copy-start | bytes 6291460 | tf_op jit(solution)/shard_map/while
  199.3 4.9 %copy-start.4 = (bf16[1024,4,128]{2,0,1:T(8,128)(2,1)S(1)}, bf16[1024,4,128]{2,0,1:T(8,128)(2,1)}, u32[]{:S(2)}) copy-start(bf16[1024,4,128]{2,0,1:T(8,128)(2,1)} %get-tuple-element.318) | copy-start | bytes 3145732 | tf_op jit(solution)/shard_map/while
  206.3 8.2 %copy-start.3 = (bf16[2,512,4,128]{3,1,2,0:T(8,128)(2,1)S(1)}, bf16[2,512,4,128]{3,1,2,0:T(8,128)(2,1)}, u32[]{:S(2)}) copy-start(bf16[2,512,4,128]{3,1,2,0:T(8,128)(2,1)} %get-tuple-element.314) | copy-start | bytes 3145732 | tf_op jit(solution)/shard_map/while
  213.2 1.3 copy-start.5
  214.5 4.8 %copy-start.6 = (bf16[1024,4,128]{2,0,1:T(8,128)(2,1)S(1)}, bf16[1024,4,128]{2,0,1:T(8,128)(2,1)}, u32[]{:S(2)}) copy-start(bf16[1024,4,128]{2,0,1:T(8,128)(2,1)} %get-tuple-element.319) | copy-start | bytes 3145732 | tf_op jit(solution)/shard_map/while
  219.3 4.9 %copy-start.1 = (f32[2,512,4,128]{3,1,2,0:T(8,128)S(1)}, f32[2,512,4,128]{3,1,2,0:T(8,128)}, u32[]{:S(2)}) copy-start(f32[2,512,4,128]{3,1,2,0:T(8,128)} %get-tuple-element.320) | copy-start | bytes 6291460 | tf_op jit(solution)/shard_map/while
  219.3 4.9 %copy-start.4 = (bf16[1024,4,128]{2,0,1:T(8,128)(2,1)S(1)}, bf16[1024,4,128]{2,0,1:T(8,128)(2,1)}, u32[]{:S(2)}) copy-start(bf16[1024,4,128]{2,0,1:T(8,128)(2,1)} %get-tuple-element.318) | copy-start | bytes 3145732 | tf_op jit(solution)/shard_map/while
  229.3 28.6 %all-to-all-start.7 = ((bf16[1024,1,4,128]{3,2,1,0:T(4,128)(2,1)}), bf16[1024,1,4,128]{3,2,1,0:T(4,128)(2,1)S(1)}, u32[]{:S(2)}, u32[]{:S(2)}) async-start(bf16[1024,1,4,128]{3,2,1,0:T(4,128)(2,1)} %copy.79), calls=%async_computation.7 | async-start | bytes 2097152 | tf_op jit(solution)/shard_map/all_to_all | solution.py:113
  257.9 29.6 %all-to-all-start.3 = ((bf16[1024,1,4,128]{3,2,1,0:T(4,128)(2,1)}), bf16[1024,1,4,128]{3,2,1,0:T(4,128)(2,1)S(1)}, u32[]{:S(2)}, u32[]{:S(2)}) async-start(bf16[1024,1,4,128]{3,2,1,0:T(4,128)(2,1)} %copy.65), calls=%async_computation.3 | async-start | bytes 2097152 | tf_op jit(solution)/shard_map/all_to_all | solution.py:112
where the time goes:
time: 295 us; the launch traced here: 290 us
  waiting for transfers between devices  135 us (46%)
  matrix products  65.3 us (22%)
  starting transfers between devices  49.4 us (17%)
  local copies, waits for them, and re-layouts  38.6 us (13%)
    sub x4, matrix products, probs_block(): raised = jnp.exp(scores - top)  27.4 us
    all_to_all x1, waiting for transfers between devices, body(): lax.all_to_all(by_group(values), 'ctx', split_axis=1, concat_axis=0, tile...  21.9 us
    all_to_all x1, waiting for transfers between devices, body(): lax.all_to_all(out_half, 'ctx', split_axis=0, concat_axis=1, tiled=True)  21.1 us
    all_to_all x1, waiting for transfers between devices, body(): lax.all_to_all(by_group(queries), 'ctx', split_axis=1, concat_axis=0, til...  21 us
    all_to_all x1, waiting for transfers between devices, body(): lax.all_to_all(by_group(key_rows), 'ctx', split_axis=1, concat_axis=0, ti...  20.3 us
    all_to_all x1, waiting for transfers between devices, body(): lax.all_to_all(tangent_half, 'ctx', split_axis=0, concat_axis=1, tiled=True)  19.6 us
    all_to_all x1, waiting for transfers between devices, body(): lax.all_to_all(by_group(tangent_queries), 'ctx', split_axis=1, concat_axi...  18.7 us
    unnamed x12, local copies, waits for them, and re-layouts  14 us
  transfers between devices with their start and end apart: 8, of which 7 were waited for; matrix products, arithmetic and copies ran while one was open for 19% of the time, Pallas kernels for 0%

commit v1 on v0

v1 whole, which is shorter than its diff:
```python
import functools

import jax
import jax.numpy as jnp
from jax import lax
from jax.experimental import pallas as pl
from jax.experimental.pallas import tpu as pltpu
from jax.sharding import PartitionSpec as P

HD = 128
ARRAYS = 6
PLACE = ((0, 1), (1, 0), (2, 0), (0, 0), (1, 1), (2, 1))


def across_first(me, step, count):
    if count % 2:
        return lax.rem(me + 1 + step, count)
    half = count // 2
    side = me // half
    other = lax.rem(step // half + 1 + side, 2)
    return other * half + lax.rem(me + step, half)


def alternating(me, step, count):
    if count % 2:
        return lax.rem(me + 1 + step, count)
    half = count // 2
    side = me // half
    other = lax.rem(step + 1 + side, 2)
    return other * half + lax.rem(me + step // 2, half)


def wait_bytes(ref, sem):
    pltpu.make_async_copy(ref, ref, sem).wait()


def kernel(n, heads, rows, per, *refs):
    inputs = refs[:ARRAYS]
    outs = refs[ARRAYS:ARRAYS + 2]
    big, res, send_sem, recv_sem, own_sem, osend_sem, orecv_sem, oown_sem = refs[ARRAYS + 2:]
    me = lax.axis_index("ctx")
    total = n * rows
    rest = total - rows
    block = per * rows
    blocks = n // per
    scale = HD ** (-0.5)

    barrier = pltpu.get_barrier_semaphore()

    @pl.loop(1, n)
    def _(step):
        pl.semaphore_signal(barrier, inc=1, device_id={"ctx": lax.rem(me + step, n)})

    def columns(device, h):
        return pl.ds(pl.multiple_of((device * heads + h) * HD, HD), HD)

    def token_rows(device):
        return pl.ds(pl.multiple_of(device * rows, rows), rows)

    def landing(a, h):
        pair, half = PLACE[a]
        return big.at[h, pair, token_rows(me), pl.ds(half * HD, HD)]

    def own_in(a, h):
        return pltpu.make_async_copy(inputs[a].at[:, columns(me, h)], landing(a, h), own_sem.at[h, a])

    @pl.loop(0, heads)
    def _(h):
        for a in range(ARRAYS):
            own_in(a, h).start()

    pl.semaphore_wait(barrier, n - 1)

    @pl.loop(0, heads)
    def _(h):
        @pl.loop(0, n)
        def _(step):
            peer = alternating(me, step, n)

            @pl.when(peer != me)
            def _():
                for a in range(ARRAYS):
                    pltpu.make_async_remote_copy(
                        src_ref=inputs[a].at[:, columns(peer, h)],
                        dst_ref=landing(a, h),
                        send_sem=send_sem.at[h],
                        recv_sem=recv_sem.at[h],
                        device_id={"ctx": peer},
                    ).start()

    def own_out(i, h):
        return pltpu.make_async_copy(
            res.at[h, i, token_rows(me)], outs[i].at[:, columns(me, h)], oown_sem.at[h, i]
        )

    @pl.loop(0, heads)
    def _(h):
        for a in range(ARRAYS):
            own_in(a, h).wait()
        wait_bytes(big.at[h, :, pl.ds(0, rest), :], recv_sem.at[h])

        @pl.loop(0, blocks)
        def _(step):
            at = across_first(me // per, step, blocks)
            mine = pl.ds(pl.multiple_of(at * block, block), block)
            queries = big[h, 0, mine, :]
            scores = lax.dot_general(
                queries[:, HD:], big[h, 1, :, :HD], (((1,), (1,)), ((), ())),
                preferred_element_type=jnp.float32,
            )
            top = jnp.max(scores, axis=-1, keepdims=True)
            raised = jnp.exp((scores - top) * scale)
            inverse = 1.0 / jnp.sum(raised, axis=-1, keepdims=True)
            raised_half = raised.astype(jnp.bfloat16)
            dscores = lax.dot_general(
                queries, big[h, 1], (((1,), (1,)), ((), ())),
                preferred_element_type=jnp.float32,
            )
            weighted = raised * dscores
            correction = jnp.sum(weighted, axis=-1, keepdims=True) * (inverse * scale)
            both = jnp.dot(raised_half, big[h, 2], preferred_element_type=jnp.float32) * inverse
            along = jnp.dot(
                weighted.astype(jnp.bfloat16), big[h, 2, :, :HD], preferred_element_type=jnp.float32
            ) * (inverse * scale)
            primal = both[:, :HD]
            res[h, 0, mine, :] = primal.astype(jnp.bfloat16)
            res[h, 1, mine, :] = (along + both[:, HD:] - correction * primal).astype(jnp.bfloat16)

            for k in range(per):
                peer = at * per + k

                @pl.when(peer != me)
                def _():
                    for i in range(2):
                        pltpu.make_async_remote_copy(
                            src_ref=res.at[h, i, token_rows(peer)],
                            dst_ref=outs[i].at[:, columns(me, h)],
                            send_sem=osend_sem.at[h],
                            recv_sem=orecv_sem,
                            device_id={"ctx": peer},
                        ).start()

                @pl.when(peer == me)
                def _():
                    for i in range(2):
                        own_out(i, h).start()

    @pl.loop(0, heads)
    def _(h):
        wait_bytes(big.at[h, :, pl.ds(0, rest), :], send_sem.at[h])
        wait_bytes(res.at[h, :, pl.ds(0, rest), :], osend_sem.at[h])
        for i in range(2):
            own_out(i, h).wait()

    wait_bytes(res.at[:, :, pl.ds(0, rest), :], orecv_sem)


def body(*arrays):
    n = lax.axis_size("ctx")
    rows, width = arrays[0].shape
    heads = width // (n * HD)
    total = n * rows
    per = 2 if n % 2 == 0 and total <= 2048 else 1
    shape = jax.ShapeDtypeStruct((rows, width), jnp.bfloat16)
    anywhere = pl.BlockSpec(memory_space=pl.ANY)
    return pl.pallas_call(
        functools.partial(kernel, n, heads, rows, per),
        out_shape=(shape, shape),
        in_specs=[anywhere] * ARRAYS,
        out_specs=(anywhere, anywhere),
        scratch_shapes=[
            pltpu.VMEM((heads, 3, total, 2 * HD), jnp.bfloat16),
            pltpu.VMEM((heads, 2, total, HD), jnp.bfloat16),
            pltpu.SemaphoreType.DMA((heads,)),
            pltpu.SemaphoreType.DMA((heads,)),
            pltpu.SemaphoreType.DMA((heads, ARRAYS)),
            pltpu.SemaphoreType.DMA((heads,)),
            pltpu.SemaphoreType.DMA,
            pltpu.SemaphoreType.DMA((heads, 2)),
        ],
        compiler_params=pltpu.CompilerParams(
            collective_id=0, has_side_effects=True, vmem_limit_bytes=50 * 2**20
        ),
        cost_estimate=pl.CostEstimate(
            flops=12 * heads * total * total * HD,
            bytes_accessed=2 * 8 * rows * width,
            transcendentals=heads * total * total,
        ),
    )(*arrays)


def solution(mesh):
    spec = P(("clip", "ctx"), None)
    return jax.shard_map(
        body, mesh=mesh, in_specs=(spec,) * ARRAYS, out_specs=(spec, spec), check_vma=False
    )
```

time: 295 us -> 191 us (0.65); the launches traced: 290 us -> 191 us
  Pallas kernels: 0 us -> 187 us
  waiting for transfers between devices: 135 us -> 0 us
  matrix products: 65.3 us -> 0 us
  starting transfers between devices: 49.4 us -> 0 us
  local copies, waits for them, and re-layouts: 38.6 us -> 3.16 us
    pallas_call x0 -> x1, Pallas kernels: none -> 187 us  [body(): pl.pallas_call(functools.partial(kernel, n, heads, rows, per), out_shape=...]
    all_to_all x8 -> x0, waiting for transfers between devices: 135 us -> none  [the longest x1 21.9 us: body(): lax.all_to_all(by_group(values), 'ctx', split_axis=1, concat_axis=0, tile...]
    all_to_all x8 -> x0, starting transfers between devices: 49.4 us -> none  [the longest x1 6.45 us: body(): lax.all_to_all(by_group(tangent_values), 'ctx', split_axis=1, concat_axis...]
    dot_general x10 -> x0, matrix products: 37.8 us -> none  [the longest x2 11.9 us: primal_block(): jnp.einsum('hqk,khd->qhd', prob_half, value_all, preferred_element_type=j...]
    sub x4 -> x0, matrix products: 27.4 us -> none  [probs_block(): raised = jnp.exp(scores - top)]
    reshape x6 -> x0, local copies, waits for them, and re-layouts: 12 us -> none  [the longest x4 7.2 us: by_group(): return array.reshape(tok_rows, groups, head_count, HD)]
    unnamed x12 -> x4, local copies, waits for them, and re-layouts: 14 us -> 3.16 us
    all_to_all x10 -> x0, local copies, waits for them, and re-layouts: 9.79 us -> none  [the longest x1 2.35 us: body(): lax.all_to_all(by_group(tangent_keys), 'ctx', split_axis=1, concat_axis=0...]
  transfers between devices with their start and end apart: 8 -> 0, of which waited for: 7 -> 0; matrix products, arithmetic and copies ran while one was open for 19% -> 0% of each run, Pallas kernels for 0% -> 0%
where the time goes in v1:
time: 191 us
  Pallas kernels  187 us (98%)
  local copies, waits for them, and re-layouts  3.16 us (2%)
    pallas_call x1, Pallas kernels, body(): pl.pallas_call(functools.partial(kernel, n, heads, rows, per), out_shape=...  187 us

profile of v1, /device:TPU:11, one launch (start us, length us, event | category | flops | bytes accessed | tf_op | source)
XLA Modules:
  0.0 190.7 jit_solution(10139323051149168297)
XLA Ops:
  0.6 0.0 copy-start
  0.6 1.2 copy-done
  1.9 186.9 %shard_map.77 = (bf16[128,4096]{1,0:T(8,128)(2,1)S(1)}, bf16[128,4096]{1,0:T(8,128)(2,1)S(1)}) custom-call(bf16[128,4096]{1,0:T(8,128)(2,1)S(1)} %copy-done, bf16[128,4096]{1,0:T(8,128)(2,1)} %refs_1_.1, bf16[128,4096]{1,0:T(8,128)(2,1)} %refs_2_.1, bf16[128,4096]{1,0:T(8,128)(2,1)} %refs_3_.1, bf16[128,4096]{1,0:T(8,128)(2,1)} %refs_4_.1, ...), custom_call_target="tpu_custom_call" | custom-call | flops 6442450944 | bytes 8388608 | tf_op jit(solution)/shard_map/pallas_call | solution.py:166
  188.8 1.0 copy.10
  189.7 1.0 copy.11
Async XLA Ops:
  0.6 1.2 copy-start

commit v2 on v1

--- a/solution.py
+++ b/solution.py
@@ -93,11 +93,39 @@
             res.at[h, i, token_rows(me)], outs[i].at[:, columns(me, h)], oown_sem.at[h, i]
         )
 
+    def send_out(peer, h):
+        @pl.when(peer != me)
+        def _():
+            for i in range(2):
+                pltpu.make_async_remote_copy(
+                    src_ref=res.at[h, i, token_rows(peer)],
+                    dst_ref=outs[i].at[:, columns(me, h)],
+                    send_sem=osend_sem.at[h],
+                    recv_sem=orecv_sem,
+                    device_id={"ctx": peer},
+                ).start()
+
+        @pl.when(peer == me)
+        def _():
+            for i in range(2):
+                own_out(i, h).start()
+
+    def send_head(h):
+        @pl.loop(0, n)
+        def _(step):
+            send_out(alternating(me, step, n), h)
+
     @pl.loop(0, heads)
     def _(h):
         for a in range(ARRAYS):
             own_in(a, h).wait()
         wait_bytes(big.at[h, :, pl.ds(0, rest), :], recv_sem.at[h])
+
+        @pl.when(h == heads - 1)
+        def _():
+            @pl.loop(1 if heads > 2 else 0, heads - 1)
+            def _(early):
+                send_head(early)
 
         @pl.loop(0, blocks)
         def _(step):
@@ -126,24 +154,14 @@
             res[h, 0, mine, :] = primal.astype(jnp.bfloat16)
             res[h, 1, mine, :] = (along + both[:, HD:] - correction * primal).astype(jnp.bfloat16)
 
-            for k in range(per):
-                peer = at * per + k
-
-                @pl.when(peer != me)
-                def _():
-                    for i in range(2):
-                        pltpu.make_async_remote_copy(
-                            src_ref=res.at[h, i, token_rows(peer)],
-                            dst_ref=outs[i].at[:, columns(me, h)],
-                            send_sem=osend_sem.at[h],
-                            recv_sem=orecv_sem,
-                            device_id={"ctx": peer},
-                        ).start()
-
-                @pl.when(peer == me)
-                def _():
-                    for i in range(2):
-                        own_out(i, h).start()
+            @pl.when(h == heads - 1)
+            def _():
+                for k in range(per):
+                    send_out(at * per + k, h)
+
+        @pl.when((h == heads - 2) & (heads > 2))
+        def _():
+            send_head(0)
 
     @pl.loop(0, heads)
     def _(h):
@@ -163,10 +181,11 @@
     per = 2 if n % 2 == 0 and total <= 2048 else 1
     shape = jax.ShapeDtypeStruct((rows, width), jnp.bfloat16)
     anywhere = pl.BlockSpec(memory_space=pl.ANY)
+    in_hbm = pl.BlockSpec(memory_space=pltpu.HBM)
     return pl.pallas_call(
         functools.partial(kernel, n, heads, rows, per),
         out_shape=(shape, shape),
-        in_specs=[anywhere] * ARRAYS,
+        in_specs=[in_hbm] * ARRAYS,
         out_specs=(anywhere, anywhere),
         scratch_shapes=[
             pltpu.VMEM((heads, 3, total, 2 * HD), jnp.bfloat16),

time: 191 us -> 195 us (1.021)
  Pallas kernels: 187 us -> 189 us
    pallas_call x1, Pallas kernels: 187 us -> 189 us  [body(): pl.pallas_call(functools.partial(kernel, n, heads, rows, per), out_shape=...]
where the time goes in v2:
time: 195 us; the launch traced here: 193 us
  Pallas kernels  189 us (97%)
  local copies, waits for them, and re-layouts  3.16 us (2%)
    pallas_call x1, Pallas kernels, body(): pl.pallas_call(functools.partial(kernel, n, heads, rows, per), out_shape=...  189 us

profile of v2, /device:TPU:11, one launch (start us, length us, event | category | flops | bytes accessed | tf_op | source)
XLA Modules:
  0.0 193.0 jit_solution(14874241528005786144)
XLA Ops:
  0.6 0.0 copy-start
  0.6 1.2 copy-done
  1.9 189.2 %shard_map.77 = (bf16[128,4096]{1,0:T(8,128)(2,1)S(1)}, bf16[128,4096]{1,0:T(8,128)(2,1)S(1)}) custom-call(bf16[128,4096]{1,0:T(8,128)(2,1)S(1)} %copy-done, bf16[128,4096]{1,0:T(8,128)(2,1)} %refs_1_.1, bf16[128,4096]{1,0:T(8,128)(2,1)} %refs_2_.1, bf16[128,4096]{1,0:T(8,128)(2,1)} %refs_3_.1, bf16[128,4096]{1,0:T(8,128)(2,1)} %refs_4_.1, ...), custom_call_target="tpu_custom_call" | custom-call | flops 6442450944 | bytes 8388608 | tf_op jit(solution)/shard_map/pallas_call | solution.py:185
  191.1 1.0 copy.10
  192.0 1.0 copy.11
Async XLA Ops:
  0.6 1.2 copy-start

commit v3 on v1

--- a/solution.py
+++ b/solution.py
@@ -71,22 +71,28 @@
 
     pl.semaphore_wait(barrier, n - 1)
 
-    @pl.loop(0, heads)
-    def _(h):
-        @pl.loop(0, n)
+    def send_in(a, peer, h):
+        pltpu.make_async_remote_copy(
+            src_ref=inputs[a].at[:, columns(peer, h)],
+            dst_ref=landing(a, h),
+            send_sem=send_sem.at[h],
+            recv_sem=recv_sem.at[h],
+            device_id={"ctx": peer},
+        ).start()
+
+    turns = 2 if n % 2 == 0 else 1
+
+    @pl.loop(0, heads)
+    def _(h):
+        @pl.loop(0, n // turns)
         def _(step):
-            peer = alternating(me, step, n)
-
-            @pl.when(peer != me)
-            def _():
-                for a in range(ARRAYS):
-                    pltpu.make_async_remote_copy(
-                        src_ref=inputs[a].at[:, columns(peer, h)],
-                        dst_ref=landing(a, h),
-                        send_sem=send_sem.at[h],
-                        recv_sem=recv_sem.at[h],
-                        device_id={"ctx": peer},
-                    ).start()
+            for a in range(ARRAYS):
+                for turn in range(turns):
+                    peer = alternating(me, step * turns + turn, n)
+
+                    @pl.when(peer != me)
+                    def _():
+                        send_in(a, peer, h)
 
     def own_out(i, h):
         return pltpu.make_async_copy(

time: 191 us -> 189 us (0.990)
  Pallas kernels: 187 us -> 185 us
where the time goes in v3:
time: 189 us
  Pallas kernels  185 us (98%)
  local copies, waits for them, and re-layouts  3.16 us (2%)
    pallas_call x1, Pallas kernels, body(): pl.pallas_call(functools.partial(kernel, n, heads, rows, per), out_shape=...  185 us

profile of v3, /device:TPU:11, one launch (start us, length us, event | category | flops | bytes accessed | tf_op | source)
XLA Modules:
  0.0 188.8 jit_solution(11567269633424807119)
XLA Ops:
  0.6 0.0 copy-start
  0.6 1.2 copy-done
  1.9 185.0 %shard_map.77 = (bf16[128,4096]{1,0:T(8,128)(2,1)S(1)}, bf16[128,4096]{1,0:T(8,128)(2,1)S(1)}) custom-call(bf16[128,4096]{1,0:T(8,128)(2,1)S(1)} %copy-done, bf16[128,4096]{1,0:T(8,128)(2,1)} %refs_1_.1, bf16[128,4096]{1,0:T(8,128)(2,1)} %refs_2_.1, bf16[128,4096]{1,0:T(8,128)(2,1)} %refs_3_.1, bf16[128,4096]{1,0:T(8,128)(2,1)} %refs_4_.1, ...), custom_call_target="tpu_custom_call" | custom-call | flops 6442450944 | bytes 8388608 | tf_op jit(solution)/shard_map/pallas_call | solution.py:172
  186.9 1.0 copy.10
  187.8 1.0 copy.11
Async XLA Ops:
  0.6 1.2 copy-start

commit v4 on v3

--- a/solution.py
+++ b/solution.py
@@ -67,7 +67,7 @@
     @pl.loop(0, heads)
     def _(h):
         for a in range(ARRAYS):
-            own_in(a, h).start()
+            own_in(a, h).start(priority=1)
 
     pl.semaphore_wait(barrier, n - 1)
 
@@ -107,7 +107,12 @@
 
         @pl.loop(0, blocks)
         def _(step):
-            at = across_first(me // per, step, blocks)
+            group = me // per
+            at = jnp.where(
+                h == heads - 1,
+                across_first(group, step, blocks),
+                alternating(group, step, blocks),
+            )
             mine = pl.ds(pl.multiple_of(at * block, block), block)
             queries = big[h, 0, mine, :]
             scores = lax.dot_general(
@@ -149,7 +154,7 @@
                 @pl.when(peer == me)
                 def _():
                     for i in range(2):
-                        own_out(i, h).start()
+                        own_out(i, h).start(priority=1)
 
     @pl.loop(0, heads)
     def _(h):
@@ -185,7 +190,7 @@
             pltpu.SemaphoreType.DMA((heads, 2)),
         ],
         compiler_params=pltpu.CompilerParams(
-            collective_id=0, has_side_effects=True, vmem_limit_bytes=50 * 2**20
+            collective_id=0, has_side_effects=True, vmem_limit_bytes=51 * 2**20
         ),
         cost_estimate=pl.CostEstimate(
             flops=12 * heads * total * total * HD,

time: 189 us -> 188 us (level)
  no operation moved by 1% of the time
where the time goes in v4:
time: 188 us
  Pallas kernels  185 us (98%)
  local copies, waits for them, and re-layouts  1.94 us (1%)
    pallas_call x1, Pallas kernels, body(): pl.pallas_call(functools.partial(kernel, n, heads, rows, per), out_shape=...  185 us

profile of v4, /device:TPU:11, one launch (start us, length us, event | category | flops | bytes accessed | tf_op | source)
XLA Modules:
  0.0 187.8 jit_solution(7334708545029278059)
XLA Ops:
  0.6 185.2 %shard_map.77 = (bf16[128,4096]{1,0:T(8,128)(2,1)S(1)}, bf16[128,4096]{1,0:T(8,128)(2,1)S(1)}) custom-call(bf16[128,4096]{1,0:T(8,128)(2,1)} %refs_0_.1, bf16[128,4096]{1,0:T(8,128)(2,1)} %refs_1_.1, bf16[128,4096]{1,0:T(8,128)(2,1)} %refs_2_.1, bf16[128,4096]{1,0:T(8,128)(2,1)} %refs_3_.1, bf16[128,4096]{1,0:T(8,128)(2,1)} %refs_4_.1, bf16[128,4096]{1,0:T(8,128)(2,1)} %refs_5_.1), custom_call_target="tpu_custom_call" | custom-call | flops 6442450944 | bytes 8388608 | tf_op jit(solution)/shard_map/pallas_call | solution.py:177
  185.9 1.0 copy.10
  186.9 1.0 copy.11

commit v5 on v4

--- a/solution.py
+++ b/solution.py
@@ -9,7 +9,6 @@
 
 HD = 128
 ARRAYS = 6
-PLACE = ((0, 1), (1, 0), (2, 0), (0, 0), (1, 1), (2, 1))
 
 
 def across_first(me, step, count):
@@ -58,8 +57,7 @@
         return pl.ds(pl.multiple_of(device * rows, rows), rows)
 
     def landing(a, h):
-        pair, half = PLACE[a]
-        return big.at[h, pair, token_rows(me), pl.ds(half * HD, HD)]
+        return big.at[h, a, token_rows(me), :]
 
     def own_in(a, h):
         return pltpu.make_async_copy(inputs[a].at[:, columns(me, h)], landing(a, h), own_sem.at[h, a])
@@ -115,8 +113,9 @@
             )
             mine = pl.ds(pl.multiple_of(at * block, block), block)
             queries = big[h, 0, mine, :]
+            both_queries = jnp.concatenate([big[h, 3, mine, :], queries], axis=-1)
             scores = lax.dot_general(
-                queries[:, HD:], big[h, 1, :, :HD], (((1,), (1,)), ((), ())),
+                queries, big[h, 1], (((1,), (1,)), ((), ())),
                 preferred_element_type=jnp.float32,
             )
             top = jnp.max(scores, axis=-1, keepdims=True)
@@ -124,14 +123,17 @@
             inverse = 1.0 / jnp.sum(raised, axis=-1, keepdims=True)
             raised_half = raised.astype(jnp.bfloat16)
             dscores = lax.dot_general(
-                queries, big[h, 1], (((1,), (1,)), ((), ())),
-                preferred_element_type=jnp.float32,
+                both_queries, jnp.concatenate([big[h, 1], big[h, 4]], axis=-1),
+                (((1,), (1,)), ((), ())), preferred_element_type=jnp.float32,
             )
             weighted = raised * dscores
             correction = jnp.sum(weighted, axis=-1, keepdims=True) * (inverse * scale)
-            both = jnp.dot(raised_half, big[h, 2], preferred_element_type=jnp.float32) * inverse
+            both = jnp.dot(
+                raised_half, jnp.concatenate([big[h, 2], big[h, 5]], axis=-1),
+                preferred_element_type=jnp.float32,
+            ) * inverse
             along = jnp.dot(
-                weighted.astype(jnp.bfloat16), big[h, 2, :, :HD], preferred_element_type=jnp.float32
+                weighted.astype(jnp.bfloat16), big[h, 2], preferred_element_type=jnp.float32
             ) * (inverse * scale)
             primal = both[:, :HD]
             res[h, 0, mine, :] = primal.astype(jnp.bfloat16)
@@ -180,7 +182,7 @@
         in_specs=[anywhere] * ARRAYS,
         out_specs=(anywhere, anywhere),
         scratch_shapes=[
-            pltpu.VMEM((heads, 3, total, 2 * HD), jnp.bfloat16),
+            pltpu.VMEM((heads, ARRAYS, total, HD), jnp.bfloat16),
             pltpu.VMEM((heads, 2, total, HD), jnp.bfloat16),
             pltpu.SemaphoreType.DMA((heads,)),
             pltpu.SemaphoreType.DMA((heads,)),

time: 188 us -> 188 us (level)
  no operation moved by 1% of the time
where the time goes in v5:
time: 188 us
  Pallas kernels  185 us (98%)
  local copies, waits for them, and re-layouts  1.94 us (1%)
    pallas_call x1, Pallas kernels, body(): pl.pallas_call(functools.partial(kernel, n, heads, rows, per), out_shape=...  185 us

profile of v5, /device:TPU:11, one launch (start us, length us, event | category | flops | bytes accessed | tf_op | source)
XLA Modules:
  0.0 187.8 jit_solution(8848902138203205328)
XLA Ops:
  0.6 185.2 %shard_map.77 = (bf16[128,4096]{1,0:T(8,128)(2,1)S(1)}, bf16[128,4096]{1,0:T(8,128)(2,1)S(1)}) custom-call(bf16[128,4096]{1,0:T(8,128)(2,1)} %refs_0_.1, bf16[128,4096]{1,0:T(8,128)(2,1)} %refs_1_.1, bf16[128,4096]{1,0:T(8,128)(2,1)} %refs_2_.1, bf16[128,4096]{1,0:T(8,128)(2,1)} %refs_3_.1, bf16[128,4096]{1,0:T(8,128)(2,1)} %refs_4_.1, bf16[128,4096]{1,0:T(8,128)(2,1)} %refs_5_.1), custom_call_target="tpu_custom_call" | custom-call | flops 6442450944 | bytes 8388608 | tf_op jit(solution)/shard_map/pallas_call | solution.py:179
  185.9 1.0 copy.10
  186.9 1.0 copy.11

commit v6 on v4

--- a/solution.py
+++ b/solution.py
@@ -98,6 +98,21 @@
         return pltpu.make_async_copy(
             res.at[h, i, token_rows(me)], outs[i].at[:, columns(me, h)], oown_sem.at[h, i]
         )
+
+    def send_out(i, peer, h):
+        @pl.when(peer != me)
+        def _():
+            pltpu.make_async_remote_copy(
+                src_ref=res.at[h, i, token_rows(peer)],
+                dst_ref=outs[i].at[:, columns(me, h)],
+                send_sem=osend_sem.at[h],
+                recv_sem=orecv_sem,
+                device_id={"ctx": peer},
+            ).start()
+
+        @pl.when(peer == me)
+        def _():
+            own_out(i, h).start(priority=1)
 
     @pl.loop(0, heads)
     def _(h):
@@ -137,24 +152,19 @@
             res[h, 0, mine, :] = primal.astype(jnp.bfloat16)
             res[h, 1, mine, :] = (along + both[:, HD:] - correction * primal).astype(jnp.bfloat16)
 
-            for k in range(per):
-                peer = at * per + k
-
-                @pl.when(peer != me)
-                def _():
+            @pl.when(h == heads - 1)
+            def _():
+                for k in range(per):
                     for i in range(2):
-                        pltpu.make_async_remote_copy(
-                            src_ref=res.at[h, i, token_rows(peer)],
-                            dst_ref=outs[i].at[:, columns(me, h)],
-                            send_sem=osend_sem.at[h],
-                            recv_sem=orecv_sem,
-                            device_id={"ctx": peer},
-                        ).start()
-
-                @pl.when(peer == me)
-                def _():
-                    for i in range(2):
-                        own_out(i, h).start(priority=1)
+                        send_out(i, at * per + k, h)
+
+        @pl.when(h < heads - 1)
+        def _():
+            @pl.loop(0, n // turns)
+            def _(step):
+                for i in range(2):
+                    for turn in range(turns):
+                        send_out(i, alternating(me, step * turns + turn, n), h)
 
     @pl.loop(0, heads)
     def _(h):

time: 188 us -> 188 us (level)
  no operation moved by 1% of the time
where the time goes in v6:
time: 188 us
  Pallas kernels  185 us (98%)
  local copies, waits for them, and re-layouts  1.94 us (1%)
    pallas_call x1, Pallas kernels, body(): pl.pallas_call(functools.partial(kernel, n, heads, rows, per), out_shape=...  185 us

profile of v6, /device:TPU:11, one launch (start us, length us, event | category | flops | bytes accessed | tf_op | source)
XLA Modules:
  0.0 187.8 jit_solution(3164860879434593394)
XLA Ops:
  0.6 185.3 %shard_map.77 = (bf16[128,4096]{1,0:T(8,128)(2,1)S(1)}, bf16[128,4096]{1,0:T(8,128)(2,1)S(1)}) custom-call(bf16[128,4096]{1,0:T(8,128)(2,1)} %refs_0_.1, bf16[128,4096]{1,0:T(8,128)(2,1)} %refs_1_.1, bf16[128,4096]{1,0:T(8,128)(2,1)} %refs_2_.1, bf16[128,4096]{1,0:T(8,128)(2,1)} %refs_3_.1, bf16[128,4096]{1,0:T(8,128)(2,1)} %refs_4_.1, bf16[128,4096]{1,0:T(8,128)(2,1)} %refs_5_.1), custom_call_target="tpu_custom_call" | custom-call | flops 6442450944 | bytes 8388608 | tf_op jit(solution)/shard_map/pallas_call | solution.py:187
  185.9 1.0 copy.10
  186.9 1.0 copy.11
